TPU v7x, 32 devices: a whole 2x2x4 slice. The times are simulated.
32 devices in a mesh: group: 2 (over y), patch: 4 (over z), visit: 2 (over x), band: 2 (over core).
Axes of the slice: x: 2, y: 2, z: 4, core: 2. Of those that a mesh axis runs over, the one named last changes fastest.
Arguments:
- template: bfloat16 [4096, 512], P(('group', 'patch')), parts along dimension 0, may hold values from -6 to 6
- science: bfloat16 [4096, 4, 512], P(('group', 'patch'), ('visit', 'band')), parts along dimension 0, may hold values from -6 to 6
- offsets: int32 [8, 4], P(('group', 'patch'), ('visit', 'band')), parts along dimension 0, may hold values from 0 to 496
- live_flags: int32 [8, 4], P(('group', 'patch'), ('visit', 'band')), parts along dimension 0, may hold values 0 or 1
- bank: bfloat16 [16, 31], replicated, may hold values from -1 to 1
- basis_index: int32 [8, 15, 2], P(('group', 'visit', 'band')), parts along dimension 0, may hold values from 0 to 15, as said below
- coeff: float32 [8, 15], P(('group', 'visit', 'band')), parts along dimension 0, may hold values from -4 to 4
- psf_profile: bfloat16 [31], replicated, may hold values from -1 to 1
Outputs:
- difference: bfloat16 [4096, 4, 512], P(('group', 'patch'), ('visit', 'band')), parts along dimension 0
- detection: float32 [4096, 512], P(('group', 'patch', 'visit', 'band')), parts along dimension 0
There are 2 independent parts, one for each index of `group`. A program takes and returns all parts, laid end to end along the dimension named above; an argument that names none is the same for every part. Nothing has to cross between parts.
Inputs may be any that keep to these rules, and one draw needn't show every extreme that they name: For each visit w, the 15 row profile indices basis_index[w, :, 0] are distinct, and so are the 15 column profile indices basis_index[w, :, 1].
All inputs are finite; a program needn't handle non-finite values. No bound on the sum of `live_flags` on one device may be relied on, other than what follows from the above.
Results may differ from a plain program's by a relative error of at most 0.0056.
Values may be sent and summed in bfloat16 or wider, within the bound.
A program may use at most 64 MiB of HBM per device.

v0:
```python
import jax
import jax.numpy as jnp
from jax import lax
from jax.sharding import PartitionSpec as P


def shifted(shard, axis, by):
    devices = lax.axis_size(axis)
    pairs = [(i, i + by) for i in range(devices) if 0 <= i + by < devices]
    return lax.ppermute(shard, axis, pairs)


def toeplitz(profile, count):
    width = profile.shape[-1]
    lead = profile.shape[:-1]
    padded = jnp.concatenate([profile, jnp.zeros(lead + (count,), profile.dtype)], axis=-1)
    tiled = jnp.tile(padded, (1,) * len(lead) + (count,))
    tiled = tiled[..., : count * (count + width - 1)]
    return tiled.reshape(lead + (count, count + width - 1))


def profiles(bank, basis_index, coeff):
    table = bank.astype(jnp.float32)
    labels = jnp.arange(table.shape[0], dtype=jnp.int32)
    pick_row = (basis_index[:, 0:1] == labels[None, :]).astype(jnp.float32)
    pick_col = (basis_index[:, 1:2] == labels[None, :]).astype(jnp.float32)
    row_raw = jnp.dot(pick_row, table, precision=lax.Precision.HIGHEST)
    col_raw = jnp.dot(pick_col, table, precision=lax.Precision.HIGHEST)
    rowprof = (coeff[:, None] * row_raw).astype(jnp.bfloat16)
    colprof = col_raw.astype(jnp.bfloat16)
    return (rowprof, colprof)


def last_blocks(padded, block, count, extra):
    pieces = [padded[..., j * block : j * block + block + extra] for j in range(count // block)]
    return jnp.stack(pieces, axis=-2)


def lead_blocks(padded, block, count, extra, axis):
    pieces = [
        lax.slice_in_dim(padded, j * block, j * block + block + extra, axis=axis)
        for j in range(count // block)
    ]
    return jnp.stack(pieces, axis=axis)


def match_tile(window, sci, rowprof, colprof, psf):
    tile_rows, tile_cols = sci.shape
    half = psf.shape[0] // 2
    extra = 2 * half
    col_block = min(128, tile_cols)
    row_block = min(128, tile_rows)
    padded = jnp.pad(window, ((0, 0), (half, half)))
    pieces = last_blocks(padded, col_block, tile_cols, extra)
    colmat = toeplitz(colprof, col_block)
    smoothed = jnp.einsum("rji,kci->krjc", pieces, colmat, preferred_element_type=jnp.float32)
    smoothed = smoothed.reshape(colprof.shape[0], window.shape[0], tile_cols).astype(jnp.bfloat16)
    stacked = lead_blocks(smoothed, row_block, tile_rows, extra, 1)
    rowmat = toeplitz(rowprof, row_block)
    matched = jnp.einsum(
        "kbi,kjic->jbc", rowmat, stacked, preferred_element_type=jnp.float32
    ).reshape(tile_rows, tile_cols)
    difference = (sci.astype(jnp.float32) - matched).astype(jnp.bfloat16)
    dpad = jnp.pad(difference, ((0, 0), (half, half)))
    dpieces = last_blocks(dpad, col_block, tile_cols, extra)
    pcol = toeplitz(psf, col_block)
    filtrow = (
        jnp.einsum("rji,ci->rjc", dpieces, pcol, preferred_element_type=jnp.float32)
        .reshape(tile_rows, tile_cols)
        .astype(jnp.bfloat16)
    )
    fpad = jnp.pad(filtrow, ((half, half), (0, 0)))
    fpieces = lead_blocks(fpad, row_block, tile_rows, extra, 0)
    prow = toeplitz(psf, row_block)
    filtered = jnp.einsum("bi,jic->jbc", prow, fpieces, preferred_element_type=jnp.float32).reshape(
        tile_rows, tile_cols
    )
    return (difference, filtered)


def split_rows(filtered, shift_rows, live):
    tile_rows = filtered.shape[0]
    rolled = jnp.roll(filtered, shift_rows, axis=0)
    rowid = jnp.arange(tile_rows, dtype=jnp.int32)
    mine = (rowid >= shift_rows).astype(jnp.float32) * live
    spilled = (rowid < shift_rows).astype(jnp.float32) * live
    return (rolled * mine[:, None], rolled * spilled[:, None], mine, spilled)


def on_device(template, science, offsets, live_flags, bank, basis_index, coeff, psf_profile):
    tile_rows = template.shape[0]
    half = bank.shape[1] // 2
    below = shifted(template, "patch", -1)
    above = shifted(template[tile_rows - half :], "patch", 1)
    stacked = jnp.concatenate([above, template, below], axis=0)
    shift_rows = offsets[0, 0]
    window = lax.dynamic_slice_in_dim(stacked, shift_rows, tile_rows + 2 * half, 0)
    rowprof, colprof = profiles(bank, basis_index[0], coeff[0])
    difference, filtered = match_tile(window, science[:, 0, :], rowprof, colprof, psf_profile)
    live = live_flags[0, 0].astype(jnp.float32)
    mine, spill, mine_cover, spill_cover = split_rows(filtered, shift_rows, live)
    spill_in, cover_in = (
        shifted(spill.astype(jnp.bfloat16), "patch", 1).astype(spill.dtype),
        shifted(spill_cover.astype(jnp.bfloat16), "patch", 1).astype(spill_cover.dtype),
    )
    accum, cover = (
        lax.psum_scatter(mine + spill_in, ("visit", "band"), scatter_dimension=0, tiled=True),
        lax.psum_scatter(mine_cover + cover_in, ("visit", "band"), scatter_dimension=0, tiled=True),
    )
    detection = accum * lax.rsqrt(jnp.maximum(cover, 1.0))[:, None]
    return (difference[:, None, :], detection)


def solution(mesh):
    return jax.shard_map(
        on_device,
        mesh=mesh,
        in_specs=(
            P(("group", "patch"), None),
            P(("group", "patch"), ("visit", "band"), None),
            P(("group", "patch"), ("visit", "band")),
            P(("group", "patch"), ("visit", "band")),
            P(),
            P(("group", "visit", "band"), None, None),
            P(("group", "visit", "band"), None),
            P(),
        ),
        out_specs=(
            P(("group", "patch"), ("visit", "band"), None),
            P(("group", "patch", "visit", "band"), None),
        ),
        check_vma=False,
    )
```

profile of v0, /device:TPU:0, one launch (start us, length us, event | category | flops | bytes accessed | tf_op | source)
XLA Modules:
  0.0 122.1 jit_solution(18085833876973116050)
XLA Ops:
  7.2 1.3 %copy.36 = bf16[512,512]{0,1:T(8,128)(2,1)S(1)} copy(bf16[512,512]{1,0:T(8,128)(2,1)} %param.8) | data formatting | bytes 1048576 | tf_op args[0]
  8.5 1.3 %collective-permute-start.1 = (bf16[512,512]{0,1:T(8,128)(2,1)S(1)}, bf16[512,512]{0,1:T(8,128)(2,1)}, u32[]{:S(2)}, u32[]{:S(2)}) collective-permute-start(bf16[512,512]{0,1:T(8,128)(2,1)S(1)} %copy.36), channel_id=1, source_target_pairs={{4,0},{8,4},{12,8},{5,1},{9,5},{13,9},{6,2},{10,6},{14,10},{7,3},{... | collective-permute-start | bytes 1572872 | tf_op jit(solution)/shard_map/ppermute | solution.py:10
  10.7 5.6 %collective-permute-start = (bf16[15,512]{0,1:T(8,128)(2,1)S(1)}, bf16[15,512]{0,1:T(8,128)(2,1)S(1)}, u32[]{:S(2)}, u32[]{:S(2)}) collective-permute-start(bf16[15,512]{0,1:T(8,128)(2,1)S(1)} %copy.34), channel_id=1, source_target_pairs={{0,4},{4,8},{8,12},{1,5},{5,9},{9,13},{2,6},{6,10},{10,14},{3,7},{... | collective-permute-start | bytes 46088 | tf_op jit(solution)/shard_map/ppermute | solution.py:10
  16.9 0.8 slice_bitcast_fusion.6
  18.5 0.8 fusion.8
  19.4 1.5 %tile.13 = bf16[15,20352]{1,0:T(8,128)(2,1)S(1)} reshape(bf16[15,128,159]{2,1,0:T(8,128)(2,1)S(1)} %tile.12) | data formatting | bytes 1221120 | tf_op jit(solution)/shard_map/tile | solution.py:17
  21.0 2.9 %reshape.55 = bf16[15,128,158]{2,1,0:T(8,128)(2,1)S(1)} reshape(bf16[15,20224]{1,0:T(8,128)(2,1)S(1)} %slice.97) | data formatting | bytes 1213440 | tf_op jit(solution)/shard_map/reshape | solution.py:19
  23.9 1.5 %tile.15 = bf16[15,20352]{1,0:T(8,128)(2,1)S(1)} reshape(bf16[15,128,159]{2,1,0:T(8,128)(2,1)S(1)} %tile.14) | data formatting | bytes 1221120 | tf_op jit(solution)/shard_map/tile | solution.py:17
  25.5 3.8 %reshape.56 = bf16[15,128,158]{2,1,0:T(8,128)(2,1)} reshape(bf16[15,20224]{1,0:T(8,128)(2,1)S(1)} %slice.102) | data formatting | bytes 1213440 | tf_op jit(solution)/shard_map/reshape | solution.py:19
  29.3 1.3 %copy.33 = bf16[512,1,512]{0,2,1:T(8,128)(2,1)S(1)} copy(bf16[512,1,512]{2,0,1:T(8,128)(2,1)} %param.9) | data formatting | bytes 1048576 | tf_op args[1]
  31.1 3.2 %concatenate.18 = bf16[1039,512]{0,1:T(8,128)(2,1)S(1)} concatenate(bf16[15,512]{0,1:T(8,128)(2,1)S(1)} %collective-permute-done, bf16[512,512]{0,1:T(8,128)(2,1)S(1)} %copy.36, bf16[512,512]{0,1:T(8,128)(2,1)} %collective-permute-done.1), dimensions={0} | concatenate | bytes 2127872 | tf_op jit(solution)/shard_map/concatenate | solution.py:95
  35.1 3.0 %convert_bitcast_fusion = bf16[15,542,4,128]{3,1,2,0:T(8,128)(2,1)S(1)} fusion(bf16[15,128,158]{2,1,0:T(8,128)(2,1)S(1)} %reshape.55, bf16[542,1,158]{0,2,1:T(8,128)(2,1)S(1)} %get-tuple-element.15, bf16[542,1,158]{0,2,1:T(8,128)(2,1)S(1)} %get-tuple-element.13, bf16[542,1,158]{0,2,1:T(8,128)(2,1)S(1)} %get-tuple-element.12, ...), kind=kOutput, calls=%fused_computation.8 | convolution fusion | flops 1322271872 | bytes 9616928 | tf_op jit(solution)/shard_map/rji,kci->krjc/dot_general | solution.py:56
  38.1 9.8 %copy.38 = bf16[15,542,4,128]{3,2,1,0:T(4,128)(2,1)} copy(bf16[15,542,4,128]{3,1,2,0:T(8,128)(2,1)S(1)} %convert_bitcast_fusion) | data formatting | bytes 16650240 | tf_op jit(solution)/shard_map/convert_element_type | solution.py:57
  47.8 12.9 %convert_element_type.69 = bf16[15,542,512]{2,1,0:T(8,128)(2,1)} reshape(bf16[15,542,4,128]{3,2,1,0:T(4,128)(2,1)} %copy.38) | data formatting | bytes 16650240 | tf_op jit(solution)/shard_map/convert_element_type | solution.py:57
  60.7 4.3 %slice_bitcast_fusion.3 = (bf16[15,1,158,512]{3,2,0,1:T(8,128)(2,1)S(1)}, bf16[15,1,158,512]{3,2,0,1:T(8,128)(2,1)S(1)}, bf16[15,1,158,512]{3,2,0,1:T(8,128)(2,1)S(1)}, bf16[15,1,158,512]{3,2,0,1:T(8,128)(2,1)S(1)}) fusion(bf16[15,542,512]{2,1,0:T(8,128)(2,1)} %convert_element_type.69), kind=kLoop, calls=%fused_computation.12 | loop fusion | bytes 19415040 | tf_op jit(solution)/shard_map/stack | solution.py:44
  65.0 2.7 %fusion = f32[4,512,128,1]{1,2,3,0:T(8,128)S(1)} fusion(bf16[15,1,158,512]{3,2,0,1:T(8,128)(2,1)S(1)} %get-tuple-element.9, bf16[15,1,158,512]{3,2,0,1:T(8,128)(2,1)S(1)} %get-tuple-element.10, bf16[15,1,158,512]{3,2,0,1:T(8,128)(2,1)S(1)} %get-tuple-element.11, bf16[15,1,158,512]{3,2,0,1:T(8,128)(2,1)S(1)} %get-tuple-element.8, ...), kind=kOutput, calls=%fused_computation | convolution fusion | flops 1257123840 | bytes 11362816 | tf_op jit(solution)/shard_map/kbi,kjic->jbc/dot_general | solution.py:60
  70.6 3.9 %collective-permute-start.2 = (bf16[512,512]{1,0:T(8,128)(2,1)S(1)}, bf16[512,512]{1,0:T(8,128)(2,1)S(1)}, u32[]{:S(2)}, u32[]{:S(2)}) collective-permute-start(bf16[512,512]{1,0:T(8,128)(2,1)S(1)} %multiply_convert_fusion), channel_id=1, source_target_pairs={{0,4},{4,8},{8,12},{1,5},{5,9},{9,13},{2,6},{6,10},{10,14},{3,7},{... | collective-permute-start | bytes 1572872 | tf_op jit(solution)/shard_map/ppermute | solution.py:10
  74.6 10.6 %collective-permute-done.2 = bf16[512,512]{1,0:T(8,128)(2,1)S(1)} collective-permute-done((bf16[512,512]{1,0:T(8,128)(2,1)S(1)}, bf16[512,512]{1,0:T(8,128)(2,1)S(1)}, u32[]{:S(2)}, u32[]{:S(2)}) %collective-permute-start.2) | collective-permute-done | bytes 524320 | tf_op jit(solution)/shard_map/ppermute | solution.py:10
  85.1 1.4 %convert_add_fusion = f32[512,512]{1,0:T(8,128)} fusion(bf16[512,512]{1,0:T(8,128)(2,1)S(1)} %collective-permute-done.2, f32[512]{0:T(512)S(1)} %fusion.46, s32[]{:T(128)S(6)} %select_n.18, f32[512,512]{1,0:T(8,128)S(1)} %bitcast.89), kind=kLoop, calls=%fused_computation.25 | loop fusion | flops 1048576 | bytes 2623492 | tf_op jit(solution)/shard_map/add | solution.py:107
  86.5 4.4 %collective-permute-start.3 = (bf16[512]{0:T(512)(128)(2,1)S(1)}, bf16[512]{0:T(512)(128)(2,1)S(1)}, u32[]{:S(2)}, u32[]{:S(2)}) collective-permute-start(bf16[512]{0:T(512)(128)(2,1)S(1)} %fusion.49), channel_id=1, source_target_pairs={{0,4},{4,8},{8,12},{1,5},{5,9},{9,13},{2,6},{6,10},{10,14},{3,7},{... | collective-permute-start | bytes 3080 | tf_op jit(solution)/shard_map/ppermute | solution.py:10
  92.2 5.7 %all-reduce.6 = f32[512]{0:T(512)S(1)} all-reduce(f32[512]{0:T(512)S(1)} %convert_add_fusion.1), channel_id=3, replica_groups=mesh['group'=2,'patch'=4,'visit'=2,'band'=2] {'visit','band'}, use_global_device_ids=true, to_apply=%region_1.2.clone | all-reduce | flops 512 | bytes 4096
  98.5 1.0 copy.48
  99.5 14.0 %reduce-scatter.2.cloned.1.call-done = f32[128,512]{1,0:T(8,128)} async-done(((f32[512,512]{1,0:T(8,128)}), f32[128,512]{1,0:T(8,128)}) %reduce-scatter.2.cloned.1.call-update) | async-done | bytes 262160 | tf_op jit(solution)/shard_map/reduce_scatter | solution.py:107
  113.5 1.7 %broadcast_multiply_fusion = f32[128,512]{1,0:T(8,128)} fusion(f32[128,512]{1,0:T(8,128)} %reduce-scatter.2.cloned.1.call-done, f32[128]{0:T(128)S(1)} %fusion.48), kind=kLoop, calls=%fused_computation.67 | loop fusion | flops 65536 | bytes 524800 | tf_op jit(solution)/shard_map/mul | solution.py:110
  (51 shorter events, 6.6 us)
Async XLA Ops:
  7.2 11.1 %copy-start = (bf16[16,31]{1,0:T(8,128)(2,1)S(1)}, bf16[16,31]{1,0:T(8,128)(2,1)}, u32[]{:S(2)}) copy-start(bf16[16,31]{1,0:T(8,128)(2,1)} %param.12) | copy-start | bytes 2980
  7.2 106.3 %reduce-scatter.2.cloned.1.call-start = ((), (), s32[]{:S(2)}) async-start(), calls=%async_computation.1 | async-start | bytes 1310720 | tf_op jit(solution)/shard_map/reduce_scatter | solution.py:107
  8.5 22.7 %collective-permute-start.1 = (bf16[512,512]{0,1:T(8,128)(2,1)S(1)}, bf16[512,512]{0,1:T(8,128)(2,1)}, u32[]{:S(2)}, u32[]{:S(2)}) collective-permute-start(bf16[512,512]{0,1:T(8,128)(2,1)S(1)} %copy.36), channel_id=1, source_target_pairs={{4,0},{8,4},{12,8},{5,1},{9,5},{13,9},{6,2},{10,6},{14,10},{7,3},{... | collective-permute-start | bytes 1572872 | tf_op jit(solution)/shard_map/ppermute | solution.py:10
  10.7 20.5 %collective-permute-start = (bf16[15,512]{0,1:T(8,128)(2,1)S(1)}, bf16[15,512]{0,1:T(8,128)(2,1)S(1)}, u32[]{:S(2)}, u32[]{:S(2)}) collective-permute-start(bf16[15,512]{0,1:T(8,128)(2,1)S(1)} %copy.34), channel_id=1, source_target_pairs={{0,4},{4,8},{8,12},{1,5},{5,9},{9,13},{2,6},{6,10},{10,14},{3,7},{... | collective-permute-start | bytes 46088 | tf_op jit(solution)/shard_map/ppermute | solution.py:10
  23.9 6.6 %copy-start.2 = (bf16[31]{0:T(256)(128)(2,1)S(1)}, bf16[31]{0:T(256)(128)(2,1)}, u32[]{:S(2)}) copy-start(bf16[31]{0:T(256)(128)(2,1)} %param.15) | copy-start | bytes 190
  60.7 4.3 %copy-start.1 = (bf16[15,128,158]{2,1,0:T(8,128)(2,1)S(1)}, bf16[15,128,158]{2,1,0:T(8,128)(2,1)}, u32[]{:S(2)}) copy-start(bf16[15,128,158]{2,1,0:T(8,128)(2,1)} %reshape.56) | copy-start | bytes 1820164
  70.2 20.7 %copy-start.3 = (u32[32]{0:T(128)S(1)}, u32[32]{0:T(128)}, u32[]{:S(2)}) copy-start(u32[32]{0:T(128)} %constant.53) | copy-start | bytes 388
  70.6 14.5 %collective-permute-start.2 = (bf16[512,512]{1,0:T(8,128)(2,1)S(1)}, bf16[512,512]{1,0:T(8,128)(2,1)S(1)}, u32[]{:S(2)}, u32[]{:S(2)}) collective-permute-start(bf16[512,512]{1,0:T(8,128)(2,1)S(1)} %multiply_convert_fusion), channel_id=1, source_target_pairs={{0,4},{4,8},{8,12},{1,5},{5,9},{9,13},{2,6},{6,10},{10,14},{3,7},{... | collective-permute-start | bytes 1572872 | tf_op jit(solution)/shard_map/ppermute | solution.py:10
  86.5 5.7 %collective-permute-start.3 = (bf16[512]{0:T(512)(128)(2,1)S(1)}, bf16[512]{0:T(512)(128)(2,1)S(1)}, u32[]{:S(2)}, u32[]{:S(2)}) collective-permute-start(bf16[512]{0:T(512)(128)(2,1)S(1)} %fusion.49), channel_id=1, source_target_pairs={{0,4},{4,8},{8,12},{1,5},{5,9},{9,13},{2,6},{6,10},{10,14},{3,7},{... | collective-permute-start | bytes 3080 | tf_op jit(solution)/shard_map/ppermute | solution.py:10
Sparse Core Ops, SparseCore 0:
  86.6 26.8 reduce-scatter.1
where the time goes:
time: 123 us; the launch traced here: 122 us
  local copies, waits for them, and re-layouts  48.7 us (40%)
  waiting for transfers between devices  24.6 us (20%)
  between operations  16.4 us (13%)
  starting transfers between devices  15.2 us (12%)
  matrix products  7.61 us (6%)
  blocking collectives  5.67 us (5%)
  other arithmetic  3.87 us (3%)
    convert_element_type x2, local copies, waits for them, and re-layouts, match_tile(): smoothed.reshape(colprof.shape[0], window.shape[0], tile_cols)  22.6 us
    ppermute x4, starting transfers between devices, shifted(): return lax.ppermute(shard, axis, pairs)  15.2 us
    reduce_scatter x1, waiting for transfers between devices, on_device(): lax.psum_scatter(mine + spill_in, ('visit', 'band'), scatter_dimension=0,...  14 us
    ppermute x4, waiting for transfers between devices, shifted(): return lax.ppermute(shard, axis, pairs)  10.6 us
    reshape x3, local copies, waits for them, and re-layouts, toeplitz(): return tiled.reshape(lead + (count, count + width - 1))  6.9 us
    unnamed x1, blocking collectives  5.67 us
    another operation x4, local copies, waits for them, and re-layouts, lead_blocks(): return jnp.stack(pieces, axis=axis)  4.52 us
    unnamed x12, local copies, waits for them, and re-layouts  4.15 us
  transfers between devices with their start and end apart: 5, of which 2 were waited for; matrix products, arithmetic and copies ran while one was open for 14% of the time, Pallas kernels for 0%

commit v1 on v0

v1 whole, which is shorter than its diff:
```python
import functools

import jax
import jax.numpy as jnp
from jax import lax
from jax.experimental import pallas as pl
from jax.experimental.pallas import tpu as pltpu
from jax.sharding import PartitionSpec as P

F32 = jnp.float32
BF16 = jnp.bfloat16
MESH = pl.DeviceIdType.MESH
GV = 16
A = 4
CB = 64


def dot(a, b):
    return jnp.dot(a, b, preferred_element_type=F32)


def dot_tn(a, b):
    return lax.dot_general(a, b, (((0,), (0,)), ((), ())), preferred_element_type=F32)


def iota(shape, axis):
    return lax.broadcasted_iota(jnp.int32, shape, axis)


def onehot(mask):
    return jnp.where(mask, 1.0, 0.0).astype(BF16)


def banded(profile, size, taps, row0, rows):
    half = taps // 2
    wide = jnp.broadcast_to(profile, (rows, size))
    rolled = pltpu.roll(wide, (row0 - half) % size, 1, stride=1, stride_axis=0)
    off = iota((rows, size), 1) - (iota((rows, size), 0) + row0)
    return jnp.where((off >= -half) & (off <= half), rolled, 0.0).astype(BF16)


def kernel(sizes, tpl, sci, off, live, bank, index, coeff, psf, diff, det,
           above, below, wts, base, tmat, rmat, eacc, ea, eb, scip, dperm, fil, land, info, pinfo,
           spill, spill_in,
           z_send, z_recv, b_send, b_recv, a_send, a_recv, i_send, i_recv,
           f_send, f_recv, s_send, s_recv):
    patches, visits, bands, taps = sizes
    peers = visits * bands
    half = taps // 2
    tr, tc = tpl.shape
    nk = index.shape[1]
    nb = bank.shape[0]
    chunk = tr // peers
    spread = tr // GV
    units = spread // A
    steps = taps - 1 + A
    g, p = lax.axis_index("group"), lax.axis_index("patch")
    v, b = lax.axis_index("visit"), lax.axis_index("band")
    me = v * bands + b

    def peer(k):
        return (g, p, k // bands, k % bands)

    barrier = pltpu.get_barrier_semaphore()
    for d in range(1, peers):
        pl.semaphore_signal(barrier, inc=1, device_id=peer((me + d) % peers), device_id_type=MESH)

    @pl.when(p > 0)
    def _():
        pl.semaphore_signal(barrier, inc=1, device_id=(g, p - 1, v, b), device_id_type=MESH)

    @pl.when(p < patches - 1)
    def _():
        pl.semaphore_signal(barrier, inc=1, device_id=(g, p + 1, v, b), device_id_type=MESH)

    pl.semaphore_wait(barrier, peers - 1 + jnp.minimum(p, 1) + jnp.minimum(patches - 1 - p, 1))

    parts = 2
    share = tr // bands
    piece = share // parts

    def z_copy(c):
        rows = pl.ds(pl.multiple_of(b * share + c * piece, 16), piece)
        return pltpu.make_async_remote_copy(
            tpl.at[rows], below.at[rows], z_send.at[c], z_recv.at[c],
            device_id=(g, p - 1, v, b), device_id_type=MESH)

    def b_copy(c):
        rows = pl.ds(pl.multiple_of(b * share + c * piece, 16), piece)
        return pltpu.make_async_remote_copy(
            below.at[rows], below.at[rows], b_send.at[c], b_recv.at[c],
            device_id=(g, p, v, 1 - b), device_id_type=MESH)

    def b_landed(c):
        rows = pl.ds(pl.multiple_of((1 - b) * share + c * piece, 16), piece)
        return pltpu.make_async_remote_copy(
            below.at[rows], below.at[rows], b_send.at[c], b_recv.at[c],
            device_id=(g, p, v, 1 - b), device_id_type=MESH)

    a_copy = pltpu.make_async_remote_copy(
        tpl.at[pl.ds(tr - 16, 16)], above, a_send, a_recv,
        device_id=(g, p + 1, v, b), device_id_type=MESH)

    @pl.when(p > 0)
    def _():
        for c in range(parts):
            z_copy(c).start()

    @pl.when(p < patches - 1)
    def _():
        a_copy.start()

    row8 = iota((8, 128), 0)
    offs = off[...]
    info[me] = jnp.where(row8 == 0, jnp.broadcast_to(offs, (8, 128)).astype(F32),
                         jnp.broadcast_to(live[...], (8, 128)).astype(F32))

    def i_copy(k, slot):
        return pltpu.make_async_remote_copy(
            info.at[slot], info.at[slot], i_send.at[k], i_recv.at[slot],
            device_id=peer(k), device_id_type=MESH)

    for d in range(1, peers):
        i_copy((me + d) % peers, me).start()

    labels = iota((nb, nk), 0)
    pick_row = onehot(labels == index[0:1, :])
    pick_col = onehot(labels == index[1:2, :])
    bk = bank[...]
    rowprof = (coeff[...] * dot_tn(bk, pick_row)).astype(BF16)
    colprof = dot_tn(pick_col, bk).astype(BF16)
    lanes = A * CB
    total = jnp.zeros((base.shape[0], lanes), F32)
    for r in range(A):
        shape = (base.shape[0], taps)
        left = dot(onehot(iota(shape, 0) == iota(shape, 1) + r), rowprof).astype(BF16)
        shape = (taps, lanes)
        right = dot(colprof, onehot(iota(shape, 1) == CB * r + taps - 1 - iota(shape, 0))).astype(BF16)
        total = total + dot(left, right)
    base[...] = total

    lane = iota((128, lanes), 1) % CB
    reach = lane - iota((128, lanes), 0) + (32 + half)
    inside = (reach >= 0) & (reach < taps)

    def weights(s, carry):
        wide = jnp.broadcast_to(base[pl.ds(s, 1), :], (128, lanes))
        rolled = pltpu.roll(wide, lanes - (32 + half), 1, stride=1, stride_axis=0)
        wts[pl.ds(pl.multiple_of(s * 128, 128), 128), :] = jnp.where(inside, rolled, 0.0).astype(BF16)
        return carry

    lax.fori_loop(0, steps, weights, 0)

    shape = (taps, tc)
    psf8 = jnp.broadcast_to(psf[...], (8, taps))
    fwd = dot(psf8, onehot(iota(shape, 1) == iota(shape, 0)))[0:1]
    rev = dot(psf8, onehot(iota(shape, 1) == taps - 1 - iota(shape, 0)))[0:1]
    for r0 in range(0, tr, 128):
        eacc[pl.ds(r0, 128), :] = banded(fwd, tc, taps, r0, 128).astype(F32)
        tmat[pl.ds(r0, 128), :] = banded(rev, tc, taps, r0, 128)
    natural = eacc[0:tr, :].astype(BF16)
    for r0 in range(0, tr, 128):
        source = iota((128, tr), 0) + r0 - offs
        source = jnp.where(source < 0, source + tr, source)
        rmat[pl.ds(r0, 128), :] = dot(onehot(iota((128, tr), 1) == source), natural).astype(BF16)

    def natural_row(f, rows, width):
        pos = iota((rows, width), 0)
        return (pos % GV) * spread + A * (pos // GV) + f

    for f in range(A):
        sel = onehot(natural_row(f, units * GV, tr) == iota((units * GV, tr), 1))
        scip[pl.ds(f * units * GV, units * GV), :] = dot(sel, sci[...]).astype(BF16)

    @pl.when(p == 0)
    def _():
        above[...] = jnp.zeros_like(above)

    @pl.when(p == patches - 1)
    def _():
        below[...] = jnp.zeros_like(below)

    @pl.when(p > 0)
    def _():
        a_copy.wait_recv()

    phase = 2 * units * GV
    for f in range(A):
        row = natural_row(f, phase, tr) + offs - half
        own = dot(onehot(row == iota((phase, tr), 1)), tpl[...])
        row = natural_row(f, phase, 16) + offs - half
        own = own + dot(onehot(row == iota((phase, 16), 1) - 16), above[...])
        eacc[pl.ds(f * phase, phase), :] = own

    @pl.when(p < patches - 1)
    def _():
        for c in range(parts):
            z_copy(c).wait_recv()
            b_copy(c).start()
        for c in range(parts):
            b_landed(c).wait_recv()

    col = iota((phase, tc), 1)
    for f in range(A):
        row = natural_row(f, phase, tr) + offs - half - tr
        got = eacc[pl.ds(f * phase, phase), :] + dot(onehot(row == iota((phase, tr), 1)), below[...])
        rows = pl.ds(f * phase, phase)
        ea[rows, :] = jnp.where(col >= 32, pltpu.roll(got, 32, 1), 0.0).astype(BF16)
        eb[rows, :] = jnp.where(col < tc - 32, pltpu.roll(got, tc - 32, 1), 0.0).astype(BF16)

    m = units * GV
    low = iota((m, 128), 1) < CB
    for blk in range(tc // 128):
        cols = slice(blk * 128, blk * 128 + 128)

        def gather(ref):
            return jnp.concatenate(
                [ref[(s % A) * phase + (s // A) * GV:(s % A) * phase + (s // A) * GV + m, cols] for s in range(steps)],
                axis=1)

        lhs = jnp.concatenate([gather(ea), gather(eb)], axis=0)
        out = dot(lhs, wts[...])
        for h in range(A // 2):
            pa = out[:m, 128 * h:128 * h + 128]
            pb = out[m:, 128 * h:128 * h + 128]
            even = jnp.where(low, pa, pltpu.roll(pb, CB, 1))
            odd = jnp.where(low, pltpu.roll(pa, CB, 1), pb)
            for f, val in ((2 * h, even), (2 * h + 1, odd)):
                rows = slice(f * m, f * m + m)
                dperm[rows, cols] = (scip[rows, cols].astype(F32) - val).astype(BF16)

    pos = iota((tr, tr), 1)
    back = (pos % GV) * spread + A * ((pos % m) // GV) + pos // m
    dnat = dot(onehot(back == iota((tr, tr), 0)), dperm[...]).astype(BF16)
    diff[...] = dnat
    filtrow = dot(dnat, tmat[...]).astype(BF16)

    def f_copy(k, slot):
        return pltpu.make_async_remote_copy(
            fil.at[k], land.at[slot], f_send.at[k], f_recv.at[slot],
            device_id=peer(k), device_id_type=MESH)

    for d in range(1, peers):
        k = (me + d) % peers
        fil[k] = dot(rmat[pl.ds(pl.multiple_of(k * chunk, 16), chunk), :], filtrow).astype(BF16)
        f_copy(k, me).start()
    land[me] = dot(rmat[pl.ds(pl.multiple_of(me * chunk, 16), chunk), :], filtrow).astype(BF16)

    for d in range(1, peers):
        i_copy((me + d) % peers, (me + d) % peers).wait_recv()

    s_copy = pltpu.make_async_remote_copy(
        spill, spill_in, s_send.at[0], s_recv.at[0], device_id=(g, p + 1, v, b), device_id_type=MESH)
    c_copy = pltpu.make_async_remote_copy(
        info, pinfo, s_send.at[1], s_recv.at[1], device_id=(g, p + 1, v, b), device_id_type=MESH)

    @pl.when(p < patches - 1)
    def _():
        c_copy.start()

    @pl.when(p == 0)
    def _():
        spill_in[...] = jnp.zeros_like(spill_in)
        pinfo[...] = jnp.zeros_like(pinfo)

    for d in range(1, peers):
        f_copy((me + d) % peers, (me + d) % peers).wait_recv()

    row = (iota((chunk, 128), 0) + me * chunk).astype(F32)
    mine, over = [], []
    for w in range(peers):
        here = row >= info[w, 0:1, :]
        lit = info[w, 1:2, :]
        mine.append(jnp.where(here, lit, 0.0))
        over.append(jnp.where(here, 0.0, lit))

    def sums(masks, cols):
        acc = masks[0] * land[0, :, cols].astype(F32)
        for w in range(1, peers):
            acc = acc + masks[w] * land[w, :, cols].astype(F32)
        return acc

    blocks = [slice(c, c + 128) for c in range(0, tc, 128)]
    for cols in blocks:
        spill[:, cols] = sums(over, cols).astype(BF16)

    @pl.when(p < patches - 1)
    def _():
        s_copy.start()

    for cols in blocks:
        det[:, cols] = sums(mine, cols)
    cover = functools.reduce(jnp.add, mine)

    @pl.when(p > 0)
    def _():
        c_copy.wait_recv()
        s_copy.wait_recv()

    for w in range(peers):
        cover = cover + jnp.where(row < pinfo[w, 0:1, :], pinfo[w, 1:2, :], 0.0)
    scale = lax.rsqrt(jnp.maximum(cover, 1.0))
    for cols in blocks:
        det[:, cols] = (det[:, cols] + spill_in[:, cols].astype(F32)) * scale

    for d in range(1, peers):
        k = (me + d) % peers
        f_copy(k, me).wait_send()
        i_copy(k, me).wait_send()

    @pl.when(p > 0)
    def _():
        for c in range(parts):
            z_copy(c).wait_send()

    @pl.when(p < patches - 1)
    def _():
        a_copy.wait_send()
        c_copy.wait_send()
        s_copy.wait_send()
        for c in range(parts):
            b_copy(c).wait_send()


def solution(mesh):
    patches, visits, bands = mesh.shape["patch"], mesh.shape["visit"], mesh.shape["band"]
    peers = visits * bands

    def on_device(template, science, offsets, live_flags, bank, basis_index, coeff, psf_profile):
        tr, tc = template.shape
        taps = bank.shape[1]
        chunk = tr // peers
        vm = pl.BlockSpec(memory_space=pltpu.VMEM)
        dma = pltpu.SemaphoreType.DMA
        steps = taps - 1 + A
        difference, detection = pl.pallas_call(
            functools.partial(kernel, (patches, visits, bands, taps)),
            out_shape=(jax.ShapeDtypeStruct((tr, tc), BF16), jax.ShapeDtypeStruct((chunk, tc), F32)),
            in_specs=[vm] * 8,
            out_specs=(vm, vm),
            scratch_shapes=[
                pltpu.VMEM((16, tc), BF16),
                pltpu.VMEM((tr, tc), BF16),
                pltpu.VMEM((steps * 128, A * CB), BF16),
                pltpu.VMEM((-(-steps // 8) * 8, A * CB), F32),
                pltpu.VMEM((tc, tc), BF16),
                pltpu.VMEM((tr, tr), BF16),
                pltpu.VMEM((2 * tr, tc), F32),
                pltpu.VMEM((2 * tr, tc), BF16),
                pltpu.VMEM((2 * tr, tc), BF16),
                pltpu.VMEM((tr, tc), BF16),
                pltpu.VMEM((tr, tc), BF16),
                pltpu.VMEM((peers, chunk, tc), BF16),
                pltpu.VMEM((peers, chunk, tc), BF16),
                pltpu.VMEM((peers, 8, 128), F32),
                pltpu.VMEM((peers, 8, 128), F32),
                pltpu.VMEM((chunk, tc), BF16),
                pltpu.VMEM((chunk, tc), BF16),
                dma((2,)), dma((2,)), dma((2,)), dma((2,)), dma, dma,
                dma((peers,)), dma((peers,)), dma((peers,)), dma((peers,)), dma((2,)), dma((2,)),
            ],
            compiler_params=pltpu.CompilerParams(
                collective_id=0, has_side_effects=True, vmem_limit_bytes=56 * 1024 * 1024),
        )(template, science[:, 0, :], offsets, live_flags, bank, basis_index[0].T, coeff, psf_profile[None, :])
        return (difference[:, None, :], detection)

    return jax.shard_map(
        on_device,
        mesh=mesh,
        in_specs=(
            P(("group", "patch"), None),
            P(("group", "patch"), ("visit", "band"), None),
            P(("group", "patch"), ("visit", "band")),
            P(("group", "patch"), ("visit", "band")),
            P(),
            P(("group", "visit", "band"), None, None),
            P(("group", "visit", "band"), None),
            P(),
        ),
        out_specs=(
            P(("group", "patch"), ("visit", "band"), None),
            P(("group", "patch", "visit", "band"), None),
        ),
        check_vma=False,
    )
```

time: 123 us -> 32.4 us (0.26)
  the two profiles are of different devices: /device:TPU:0 before, /device:TPU:17 now
where the time goes in v1:
time: 32.4 us; the launch traced here: 32.2 us
  Pallas kernels  27.6 us (85%)
  local copies, waits for them, and re-layouts  2.62 us (8%)
  between operations  1.94 us (6%)
    pallas_call x1, Pallas kernels, on_device(): pl.pallas_call(functools.partial(kernel, (patches, visits, bands, taps)),...  27.6 us
    unnamed x4, local copies, waits for them, and re-layouts  2.62 us

profile of v1, /device:TPU:17, one launch (start us, length us, event | category | flops | bytes accessed | tf_op | source)
XLA Modules:
  0.0 32.2 jit_solution(8181180771167062880)
XLA Ops:
  1.9 27.6 %shard_map.95 = (bf16[512,512]{1,0:T(8,128)(2,1)}, f32[128,512]{1,0:T(8,128)}) custom-call(bf16[512,512]{1,0:T(8,128)(2,1)} %tpl.1, bf16[512,512]{1,0:T(8,128)(2,1)} %bitcast.6, s32[1,1]{1,0:T(1,128)S(6)} %copy.12.off, s32[1,1]{1,0:T(1,128)S(6)} %copy.13.live, bf16[16,31]{1,0:T(8,128)(2,1)} %bank.1, s32[2,15]{1,0:T(2,128)} %bitcast.8, f32[1,15]{1,0:T(1,128)} %coeff.1, ...), custom_call_target="tpu_custom_call" | custom-call | tf_op jit(solution)/shard_map/pallas_call | solution.py:336
  29.6 0.0 copy-start
  29.6 1.9 %copy.14 = bf16[512,1,512]{2,0,1:T(8,128)(2,1)} copy(bf16[512,1,512]{2,0,1:T(8,128)(2,1)} %bitcast.7) | data formatting | bytes 1048576
  31.5 0.0 copy-done
  31.5 0.7 %copy.15 = f32[128,512]{1,0:T(8,128)} copy(f32[128,512]{1,0:T(8,128)S(1)} %copy-done) | data formatting | bytes 524288
Async XLA Ops:
  29.6 1.9 %copy-start = (f32[128,512]{1,0:T(8,128)S(1)}, f32[128,512]{1,0:T(8,128)}, u32[]{:S(2)}) copy-start(f32[128,512]{1,0:T(8,128)} %get-tuple-element.9) | copy-start | bytes 786436

commit v2 on v1

--- a/solution.py
+++ b/solution.py
@@ -43,7 +43,7 @@
            above, below, wts, base, tmat, rmat, eacc, ea, eb, scip, dperm, fil, land, info, pinfo,
            spill, spill_in,
            z_send, z_recv, b_send, b_recv, a_send, a_recv, i_send, i_recv,
-           f_send, f_recv, s_send, s_recv):
+           f_send, f_recv, s_send, s_recv, c_send, c_recv):
     patches, visits, bands, taps = sizes
     peers = visits * bands
     half = taps // 2
@@ -209,6 +209,38 @@
         eb[rows, :] = jnp.where(col < tc - 32, pltpu.roll(got, tc - 32, 1), 0.0).astype(BF16)
 
     m = units * GV
+    pos = iota((tr, tr), 1)
+    back = (pos % GV) * spread + A * ((pos % m) // GV) + pos // m
+    back = onehot(back == iota((tr, tr), 0))
+
+    blocks = tc // 128
+
+    def cols_of(c):
+        return pl.ds(c * 128, 128)
+
+    def chunk_of(k):
+        return pl.ds(pl.multiple_of(k * chunk, 16), chunk)
+
+    def f_copy(c, k, slot):
+        return pltpu.make_async_remote_copy(
+            fil.at[c, chunk_of(k)], land.at[c, slot], f_send.at[c, k], f_recv.at[c, slot],
+            device_id=peer(k), device_id_type=MESH)
+
+    others = [lax.rem(v + d, visits) for d in range(1, visits)]
+    ranks = [to * bands + lax.rem(b + d, bands) for to in others for d in range(bands)]
+    ranks += [v * bands + lax.rem(b + d, bands) for d in range(1, bands)]
+
+    def filters(first, last):
+        lo, hi = max(first - 1, 0) * 128, min(last + 1, blocks) * 128
+        filtrow = dot(diff[:, lo:hi], tmat[lo:hi, first * 128:last * 128]).astype(BF16)
+        rolled = dot(rmat[...], filtrow).astype(BF16)
+        for c in range(first, last):
+            fil[c] = rolled[:, (c - first) * 128:(c - first) * 128 + 128]
+            for k in ranks:
+                f_copy(c, k, me).start()
+            land[c, me] = fil[c, chunk_of(me), :]
+
+    m = units * GV
     low = iota((m, 128), 1) < CB
     for blk in range(tc // 128):
         cols = slice(blk * 128, blk * 128 + 128)
@@ -228,31 +260,21 @@
             for f, val in ((2 * h, even), (2 * h + 1, odd)):
                 rows = slice(f * m, f * m + m)
                 dperm[rows, cols] = (scip[rows, cols].astype(F32) - val).astype(BF16)
-
-    pos = iota((tr, tr), 1)
-    back = (pos % GV) * spread + A * ((pos % m) // GV) + pos // m
-    dnat = dot(onehot(back == iota((tr, tr), 0)), dperm[...]).astype(BF16)
-    diff[...] = dnat
-    filtrow = dot(dnat, tmat[...]).astype(BF16)
-
-    def f_copy(k, slot):
-        return pltpu.make_async_remote_copy(
-            fil.at[k], land.at[slot], f_send.at[k], f_recv.at[slot],
-            device_id=peer(k), device_id_type=MESH)
-
-    for d in range(1, peers):
-        k = (me + d) % peers
-        fil[k] = dot(rmat[pl.ds(pl.multiple_of(k * chunk, 16), chunk), :], filtrow).astype(BF16)
-        f_copy(k, me).start()
-    land[me] = dot(rmat[pl.ds(pl.multiple_of(me * chunk, 16), chunk), :], filtrow).astype(BF16)
+        if blk % 2:
+            pair = slice((blk - 1) * 128, (blk + 1) * 128)
+            diff[:, pair] = dot(back, dperm[:, pair]).astype(BF16)
+            filters(max(blk - 2, 0), blocks if blk == blocks - 1 else blk)
 
     for d in range(1, peers):
         i_copy((me + d) % peers, (me + d) % peers).wait_recv()
 
-    s_copy = pltpu.make_async_remote_copy(
-        spill, spill_in, s_send.at[0], s_recv.at[0], device_id=(g, p + 1, v, b), device_id_type=MESH)
+    def s_copy(c):
+        return pltpu.make_async_remote_copy(
+            spill.at[c], spill_in.at[c], s_send.at[c], s_recv.at[c],
+            device_id=(g, p + 1, v, b), device_id_type=MESH)
+
     c_copy = pltpu.make_async_remote_copy(
-        info, pinfo, s_send.at[1], s_recv.at[1], device_id=(g, p + 1, v, b), device_id_type=MESH)
+        info, pinfo, c_send, c_recv, device_id=(g, p + 1, v, b), device_id_type=MESH)
 
     @pl.when(p < patches - 1)
     def _():
@@ -262,9 +284,6 @@
     def _():
         spill_in[...] = jnp.zeros_like(spill_in)
         pinfo[...] = jnp.zeros_like(pinfo)
-
-    for d in range(1, peers):
-        f_copy((me + d) % peers, (me + d) % peers).wait_recv()
 
     row = (iota((chunk, 128), 0) + me * chunk).astype(F32)
     mine, over = [], []
@@ -274,39 +293,42 @@
         mine.append(jnp.where(here, lit, 0.0))
         over.append(jnp.where(here, 0.0, lit))
 
-    def sums(masks, cols):
-        acc = masks[0] * land[0, :, cols].astype(F32)
+    def sums(masks, c):
+        acc = masks[0] * land[c, 0].astype(F32)
         for w in range(1, peers):
-            acc = acc + masks[w] * land[w, :, cols].astype(F32)
+            acc = acc + masks[w] * land[c, w].astype(F32)
         return acc
 
-    blocks = [slice(c, c + 128) for c in range(0, tc, 128)]
-    for cols in blocks:
-        spill[:, cols] = sums(over, cols).astype(BF16)
-
-    @pl.when(p < patches - 1)
-    def _():
-        s_copy.start()
-
-    for cols in blocks:
-        det[:, cols] = sums(mine, cols)
+    for c in range(blocks):
+        for k in ranks:
+            f_copy(c, k, k).wait_recv()
+        spill[c] = sums(over, c).astype(BF16)
+
+        @pl.when(p < patches - 1)
+        def _():
+            s_copy(c).start()
+
+        det[:, cols_of(c)] = sums(mine, c)
     cover = functools.reduce(jnp.add, mine)
 
     @pl.when(p > 0)
     def _():
         c_copy.wait_recv()
-        s_copy.wait_recv()
 
     for w in range(peers):
         cover = cover + jnp.where(row < pinfo[w, 0:1, :], pinfo[w, 1:2, :], 0.0)
     scale = lax.rsqrt(jnp.maximum(cover, 1.0))
-    for cols in blocks:
-        det[:, cols] = (det[:, cols] + spill_in[:, cols].astype(F32)) * scale
-
-    for d in range(1, peers):
-        k = (me + d) % peers
-        f_copy(k, me).wait_send()
+    for c in range(blocks):
+        @pl.when(p > 0)
+        def _():
+            s_copy(c).wait_recv()
+
+        det[:, cols_of(c)] = (det[:, cols_of(c)] + spill_in[c].astype(F32)) * scale
+
+    for k in ranks:
         i_copy(k, me).wait_send()
+        for c in range(blocks):
+            f_copy(c, k, me).wait_send()
 
     @pl.when(p > 0)
     def _():
@@ -317,7 +339,8 @@
     def _():
         a_copy.wait_send()
         c_copy.wait_send()
-        s_copy.wait_send()
+        for c in range(blocks):
+            s_copy(c).wait_send()
         for c in range(parts):
             b_copy(c).wait_send()
 
@@ -330,6 +353,7 @@
         tr, tc = template.shape
         taps = bank.shape[1]
         chunk = tr // peers
+        blocks = tc // 128
         vm = pl.BlockSpec(memory_space=pltpu.VMEM)
         dma = pltpu.SemaphoreType.DMA
         steps = taps - 1 + A
@@ -350,14 +374,15 @@
                 pltpu.VMEM((2 * tr, tc), BF16),
                 pltpu.VMEM((tr, tc), BF16),
                 pltpu.VMEM((tr, tc), BF16),
-                pltpu.VMEM((peers, chunk, tc), BF16),
-                pltpu.VMEM((peers, chunk, tc), BF16),
+                pltpu.VMEM((blocks, tr, 128), BF16),
+                pltpu.VMEM((blocks, peers, chunk, 128), BF16),
                 pltpu.VMEM((peers, 8, 128), F32),
                 pltpu.VMEM((peers, 8, 128), F32),
-                pltpu.VMEM((chunk, tc), BF16),
-                pltpu.VMEM((chunk, tc), BF16),
+                pltpu.VMEM((blocks, chunk, 128), BF16),
+                pltpu.VMEM((blocks, chunk, 128), BF16),
                 dma((2,)), dma((2,)), dma((2,)), dma((2,)), dma, dma,
-                dma((peers,)), dma((peers,)), dma((peers,)), dma((peers,)), dma((2,)), dma((2,)),
+                dma((peers,)), dma((peers,)), dma((blocks, peers)), dma((blocks, peers)),
+                dma((blocks,)), dma((blocks,)), dma, dma,
             ],
             compiler_params=pltpu.CompilerParams(
                 collective_id=0, has_side_effects=True, vmem_limit_bytes=56 * 1024 * 1024),

time: 32.4 us -> 32.3 us (level)
  the two profiles are of different devices: /device:TPU:17 before, /device:TPU:0 now
where the time goes in v2:
time: 32.3 us; the launch traced here: 32.1 us
  Pallas kernels  27.5 us (85%)
  local copies, waits for them, and re-layouts  2.62 us (8%)
  between operations  1.94 us (6%)
    pallas_call x1, Pallas kernels, on_device(): pl.pallas_call(functools.partial(kernel, (patches, visits, bands, taps)),...  27.5 us
    unnamed x4, local copies, waits for them, and re-layouts  2.62 us

profile of v2, /device:TPU:0, one launch (start us, length us, event | category | flops | bytes accessed | tf_op | source)
XLA Modules:
  0.0 32.1 jit_solution(7565705750792509857)
XLA Ops:
  1.9 27.5 %shard_map.95 = (bf16[512,512]{1,0:T(8,128)(2,1)}, f32[128,512]{1,0:T(8,128)}) custom-call(bf16[512,512]{1,0:T(8,128)(2,1)} %tpl.1, bf16[512,512]{1,0:T(8,128)(2,1)} %bitcast.6, s32[1,1]{1,0:T(1,128)S(6)} %copy.12.off, s32[1,1]{1,0:T(1,128)S(6)} %copy.13.live, bf16[16,31]{1,0:T(8,128)(2,1)} %bank.1, s32[2,15]{1,0:T(2,128)} %bitcast.8, f32[1,15]{1,0:T(1,128)} %coeff.1, ...), custom_call_target="tpu_custom_call" | custom-call | tf_op jit(solution)/shard_map/pallas_call | solution.py:360
  29.4 0.0 copy-start
  29.5 1.9 %copy.14 = bf16[512,1,512]{2,0,1:T(8,128)(2,1)} copy(bf16[512,1,512]{2,0,1:T(8,128)(2,1)} %bitcast.7) | data formatting | bytes 1048576
  31.4 0.0 copy-done
  31.4 0.7 %copy.15 = f32[128,512]{1,0:T(8,128)} copy(f32[128,512]{1,0:T(8,128)S(1)} %copy-done) | data formatting | bytes 524288
Async XLA Ops:
  29.4 1.9 %copy-start = (f32[128,512]{1,0:T(8,128)S(1)}, f32[128,512]{1,0:T(8,128)}, u32[]{:S(2)}) copy-start(f32[128,512]{1,0:T(8,128)} %get-tuple-element.9) | copy-start | bytes 786436
